TPU v7x, 32 devices: a whole 2x2x4 slice. The times are simulated.
32 devices in a mesh: hyp: 4 (over z), row: 2 (over x), col: 4 (over y, core).
Axes of the slice: x: 2, y: 2, z: 4, core: 2. Of those that a mesh axis runs over, the one named last changes fastest.
Arguments:
- front_orig: bfloat16 [40960, 10240], P(('hyp', 'row'), 'col'), parts along dimension 0, as said below
- child_updates: bfloat16 [65536, 8192], P(('hyp', 'row'), 'col'), parts along dimension 0, as said below
- child_map: int32 [8, 64], P('hyp'), parts along dimension 0, may hold values from 0 to 79, as said below
- panel_inverse: bfloat16 [1024, 256], P('hyp'), parts along dimension 0, as said below
Outputs:
- schur: bfloat16 [40960, 10240], P(('hyp', 'row'), 'col'), parts along dimension 0
- panel: bfloat16 [40960, 256], P(('hyp', 'row')), parts along dimension 0
There are 4 independent parts, one for each index of `hyp`. A program takes and returns all parts, laid end to end along the dimension named above; each array names one. Nothing has to cross between parts.
Inputs may be any that keep to these rules, and one draw needn't show every extreme that they name: `child_map`: each child's entries are distinct. Parent block p lies on row index p // 40 and column index p // 20. Of the 64 blocks of a child on one row index (child c on row indices c * 1 to (c + 1) - 1, in order), at most 32 lie on one parent row index; of the 16 blocks on one column index, at most 4 lie on one parent column index. Every parent row index receives the same number of blocks of each child. `child_updates`: each child's update block is symmetric. `front_orig`: Symmetric. `panel_inverse`: upper triangular with a positive diagonal.
All inputs are finite; a program needn't handle non-finite values.
Results may differ from a plain program's by a relative error of at most 0.0052.
Values may be sent and summed in bfloat16 or wider, within the bound.
A program may use at most 256 MiB of HBM per device.

v0:
```python
import jax
import jax.numpy as jnp
from jax import lax
from jax.sharding import PartitionSpec as P

B = 128
PANEL = 256


def from_root(shard, axis, root):
    mine = lax.axis_index(axis) == root
    return lax.psum(jnp.where(mine, shard, jnp.zeros_like(shard)), axis)


def one_hot(indices, columns):
    return (indices[..., None] == jnp.arange(columns, dtype=jnp.int32)).astype(jnp.bfloat16)


def earlier_same(labels):
    length = labels.shape[-1]
    matches = labels[..., :, None] == labels[..., None, :]
    before = jnp.arange(length)[None, :] < jnp.arange(length)[:, None]
    return jnp.sum(matches & before, axis=-1)


def send_table(block_ids, owner_width, capacity, owners_count):
    owners = block_ids // owner_width
    slots = owners * capacity + earlier_same(owners)
    return one_hot(slots, owners_count * capacity)


def receive_table(all_ids, owner_width, my_index, capacity):
    owners = all_ids // owner_width
    rank_in = earlier_same(owners)
    local_block = all_ids - my_index * owner_width
    arrives = (owners == my_index)[:, :, None, None]
    slot_match = rank_in[:, :, None, None] == jnp.arange(capacity)[None, None, :, None]
    block_match = local_block[:, :, None, None] == jnp.arange(owner_width)[None, None, None, :]
    table = jnp.sum(arrives & slot_match & block_match, axis=1)
    return table.reshape(-1, owner_width).astype(jnp.bfloat16)


def local(front_orig, child_updates, child_map, panel_inverse):
    n_row = lax.axis_size("row")
    n_col = lax.axis_size("col")
    me_row = lax.axis_index("row")
    me_col = lax.axis_index("col")
    rows_local, cols_local = child_updates.shape
    part_rows, part_cols = front_orig.shape
    senders = n_row // 2
    child_index = me_row // senders
    blocks_row = rows_local // B
    blocks_col = cols_local // B
    fine_count = max(n_row, n_col)
    parent_row_blocks = part_rows // B
    parent_col_blocks = part_cols // B
    row_cap = max(1, blocks_row // fine_count) * (fine_count // n_row)
    col_cap = max(1, blocks_col // fine_count) * (fine_count // n_col)
    my_map = lax.dynamic_index_in_dim(child_map, child_index, 0, keepdims=False)
    flat_map = child_map.reshape(-1)
    row_ids = lax.dynamic_slice_in_dim(flat_map, me_row * blocks_row, blocks_row)
    row_send = send_table(row_ids, parent_row_blocks, row_cap, n_row)
    row_receive = receive_table(
        child_map.reshape(n_row, blocks_row), parent_row_blocks, me_row, row_cap
    )
    col_ids = lax.dynamic_slice_in_dim(my_map, me_col * blocks_col, blocks_col)
    col_send = send_table(col_ids, parent_col_blocks, col_cap, n_col).reshape(
        blocks_col, n_col, col_cap
    )
    row_pick = row_send.reshape(blocks_row, n_row, row_cap)
    tiles_four = child_updates.reshape(blocks_row, B, blocks_col, B)
    outgoing = jnp.einsum(
        "ibjc,ipa,jqe->pqabec", tiles_four, row_pick, col_send, preferred_element_type=jnp.float32
    ).astype(jnp.bfloat16)
    outgoing = outgoing.reshape(n_row * n_col, row_cap * B, col_cap * B)
    incoming = lax.all_to_all(outgoing, ("row", "col"), split_axis=0, concat_axis=0, tiled=True)
    tiles = incoming.reshape(n_row, n_col, row_cap, B, col_cap, B)
    col_tables = jnp.stack(
        [
            receive_table(
                child_map[k].reshape(n_col, blocks_col), parent_col_blocks, me_col, col_cap
            ).reshape(n_col, col_cap, parent_col_blocks)
            for k in range(2)
        ]
    )
    per_source = jnp.repeat(col_tables, senders, axis=0)
    placed_cols = jnp.einsum(
        "rsabec,rseq->rabqc", tiles, per_source, preferred_element_type=jnp.float32
    ).astype(jnp.bfloat16)
    row_table = row_receive.reshape(n_row, row_cap, parent_row_blocks)
    assembled = jnp.einsum(
        "rabqc,rap->pbqc", placed_cols, row_table, preferred_element_type=jnp.float32
    )
    front32 = assembled.reshape(part_rows, part_cols) + front_orig.astype(jnp.float32)
    front = front32.astype(jnp.bfloat16)
    local_panel = jnp.dot(
        front[:, :PANEL], panel_inverse, preferred_element_type=jnp.float32
    ).astype(jnp.bfloat16)
    row_panel = from_root(local_panel, "col", 0)
    all_panel = lax.all_gather(row_panel, "row", axis=0, tiled=True)
    col_panel = lax.dynamic_slice_in_dim(all_panel, me_col * part_cols, part_cols, 0)
    update = lax.dot_general(
        row_panel, col_panel, (((1,), (1,)), ((), ())), preferred_element_type=jnp.float32
    )
    schur = (front.astype(jnp.float32) - update).astype(jnp.bfloat16)
    return (schur, row_panel)


def solution(mesh):
    in_specs = (P(("hyp", "row"), "col"), P(("hyp", "row"), "col"), P("hyp", None), P("hyp", None))
    out_specs = (P(("hyp", "row"), "col"), P(("hyp", "row"), None))
    return jax.shard_map(local, mesh=mesh, in_specs=in_specs, out_specs=out_specs, check_vma=False)
```

profile of v0, /device:TPU:0, one launch (start us, length us, event | category | flops | bytes accessed | tf_op | source)
XLA Modules:
  0.0 1107.1 jit_solution(13410336306181825943)
XLA Ops:
  7.2 0.8 reshape.344
  8.0 0.8 bitcast_select_fusion
  8.8 0.2 convert_reduce_fusion.7
  9.0 0.1 and_select_fusion
  9.1 0.2 convert_reduce_fusion.4
  9.2 0.1 multiply_add_fusion.3
  9.3 23.1 %copy.34 = bf16[1024,8,16,128]{3,2,1,0:T(8,128)(2,1)} copy(bf16[1024,8,16,128]{3,1,2,0:T(8,128)(2,1)} %bitcast.85) | data formatting | bytes 67108864
  32.4 39.2 %fusion.8 = bf16[2,32,128,16,128,1]{4,1,3,2,0,5:T(8,128)(2,1)} fusion(bf16[64,128,16,128]{3,2,1,0:T(8,128)(2,1)} %bitcast.83, s32[2,32]{1,0:T(2,128)S(1)} %multiply_add_fusion.1, s32[64]{0:T(128)S(1)} %multiply_add_fusion.3), kind=kOutput, calls=%fused_computation.11 | convolution fusion | flops 2147487744 | bytes 67109376 | tf_op jit(solution)/shard_map/ibjc,ipa,jqe->pqabec/dot_general | solution.py:72
  71.6 43.9 %convert_bitcast_fusion = bf16[2,4,32,128,4,128]{5,4,1,3,2,0:T(4,128)(2,1)} fusion(bf16[2,32,128,16,128,1]{4,1,3,2,0,5:T(8,128)(2,1)} %fusion.8, s32[4,4]{1,0:T(4,128)S(1)} %multiply_add_fusion, s32[16]{0:T(128)S(1)} %multiply_add_fusion.2), kind=kOutput, calls=%fused_computation.10 | convolution fusion | flops 536871168 | bytes 67108992 | tf_op jit(solution)/shard_map/ibjc,ipa,jqe->pqabec/dot_general | solution.py:72
  115.5 40.2 %copy.17 = bf16[2,4,32,128,4,128]{3,2,5,4,1,0:T(8,128)(2,1)} copy(bf16[2,4,32,128,4,128]{5,4,1,3,2,0:T(4,128)(2,1)} %convert_bitcast_fusion) | data formatting | bytes 67108864 | tf_op jit(solution)/shard_map/convert_element_type | solution.py:74
  155.7 49.3 %reshape.346 = bf16[8,4096,512]{1,2,0:T(8,128)(2,1)} reshape(bf16[2,4,32,128,4,128]{3,2,5,4,1,0:T(8,128)(2,1)} %copy.17) | data formatting | bytes 67108864 | tf_op jit(solution)/shard_map/reshape | solution.py:75
  205.0 7.2 all-to-all-start
  212.5 0.1 and.182
  212.9 0.3 convert_reduce_fusion.6
  213.3 0.1 convert_reduce_fusion.1
  213.5 0.1 convert_reduce_fusion.2
  213.7 0.2 convert_reduce_fusion.3
  213.9 1.2 convert_reduce_fusion
  215.1 360.6 %all-to-all-done = bf16[8,4096,512]{1,2,0:T(8,128)(2,1)} async-done(((bf16[8,4096,512]{1,2,0:T(8,128)(2,1)}), bf16[8,4096,512]{1,2,0:T(8,128)(2,1)}, u32[]{:S(2)}, u32[]{:S(2)}) %all-to-all-start) | async-done | bytes 33554464 | tf_op jit(solution)/shard_map/all_to_all | solution.py:76
  575.6 23.1 %copy.35 = bf16[512,8,32,128]{3,2,1,0:T(8,128)(2,1)} copy(bf16[512,8,32,128]{3,1,2,0:T(8,128)(2,1)} %bitcast.31) | data formatting | bytes 67108864
  598.7 41.7 %copy.18 = bf16[2,4,32,128,4,128]{5,4,1,3,2,0:T(4,128)(2,1)} copy(bf16[2,4,32,128,4,128]{3,2,5,4,1,0:T(8,128)(2,1)} %bitcast.84) | data formatting | bytes 67108864 | tf_op jit(solution)/shard_map/reshape | solution.py:77
  640.4 37.0 %fusion.2 = bf16[2,32,128,20,128]{4,3,2,1,0:T(8,128)(2,1)} fusion(bf16[2,4,32,128,4,128]{5,4,1,3,2,0:T(4,128)(2,1)} %copy.18, bf16[2,4,4,20,1,1]{3,2,1,5,4,0:T(4,128)(2,1)S(1)} %maximum_bitcast_fusion.4), kind=kOutput, calls=%fused_computation.6 | convolution fusion | flops 692060160 | bytes 75498752 | tf_op jit(solution)/shard_map/rsabec,rseq->rabqc/dot_general | solution.py:87
  677.4 109.5 %copy.28 = bf16[2,32,128,20,128]{2,1,0,4,3:T(8,128)(2,1)} copy(bf16[2,32,128,20,128]{4,3,2,1,0:T(8,128)(2,1)} %fusion.2) | data formatting | bytes 83886080 | tf_op jit(solution)/shard_map/convert_element_type | solution.py:89
  786.9 32.3 %fusion.17 = f32[40,128,20,128,1]{1,0,4,3,2:T(8,128)} fusion(bf16[2,32,128,20,128]{2,1,0,4,3:T(8,128)(2,1)} %copy.28, s32[2,32,40]{2,1,0:T(8,128)S(1)} %convert_reduce_fusion), kind=kOutput, calls=%fused_computation.31 | convolution fusion | flops 1677724160 | bytes 94382080 | tf_op jit(solution)/shard_map/rabqc,rap->pbqc/dot_general | solution.py:91
  819.2 35.3 %copy.49 = f32[320,8,40,128]{3,1,2,0:T(8,128)} copy(f32[320,8,40,128]{3,2,1,0:T(8,128)} %bitcast.81) | data formatting | bytes 104857600
  854.5 52.2 %copy.21 = f32[5120,2560]{1,0:T(8,128)} copy(f32[5120,2560]{0,1:T(8,128)} %bitcast.82) | data formatting | bytes 104857600 | tf_op jit(solution)/shard_map/reshape | solution.py:94
  906.6 34.2 %add_convert_fusion = bf16[5120,2560]{1,0:T(8,128)(2,1)} fusion(f32[5120,2560]{1,0:T(8,128)} %copy.21, bf16[5120,2560]{1,0:T(8,128)(2,1)} %param.4), kind=kLoop, calls=%fused_computation.5 | loop fusion | flops 39321600 | bytes 104857600 | tf_op jit(solution)/shard_map/convert_element_type | solution.py:95
  940.8 4.1 fusion.11
  945.0 61.2 %all-reduce.2.cloned.1.call-done = bf16[5120,256]{1,0:T(8,128)(2,1)} async-done(((bf16[5120,256]{1,0:T(8,128)(2,1)}), bf16[5120,256]{1,0:T(8,128)(2,1)}) %all-reduce.2.cloned.1.call-update) | async-done | bytes 2621456 | tf_op jit(solution)/shard_map/psum | solution.py:12
  1006.2 70.2 %all-gather.2.cloned.1.call-done = bf16[10240,256]{1,0:T(8,128)(2,1)} async-done(((bf16[5120,256]{1,0:T(8,128)(2,1)}), bf16[10240,256]{1,0:T(8,128)(2,1)}) %all-gather.2.cloned.1.call-update) | async-done | bytes 5242896 | tf_op jit(solution)/shard_map/all_gather | solution.py:100
  1076.3 22.4 %subtract_convert_fusion = bf16[5120,2560]{1,0:T(8,128)(2,1)} fusion(bf16[5120,2560]{1,0:T(8,128)(2,1)} %add_convert_fusion, bf16[5120,256]{1,0:T(8,128)(2,1)} %all-reduce.2.cloned.1.call-done, bf16[10240,256]{1,0:T(8,128)(2,1)} %all-gather.2.cloned.1.call-done, s32[]{:T(128)S(6)} %select_n.98), kind=kOutput, calls=%fused_computation.4 | convolution fusion | flops 6750208000 | bytes 56360964 | tf_op jit(solution)/shard_map/dot_general | solution.py:102
  1098.8 1.5 copy.51
  (35 shorter events, 0.9 us)
Async XLA Ops:
  7.2 933.6 %copy-start = (bf16[256,256]{1,0:T(8,128)(2,1)S(1)}, bf16[256,256]{1,0:T(8,128)(2,1)}, u32[]{:S(2)}) copy-start(bf16[256,256]{1,0:T(8,128)(2,1)} %param.7) | copy-start | bytes 393220
  205.0 7.3 copy-start.2
  205.0 370.6 %all-to-all-start = ((bf16[8,4096,512]{1,2,0:T(8,128)(2,1)}), bf16[8,4096,512]{1,2,0:T(8,128)(2,1)}, u32[]{:S(2)}, u32[]{:S(2)}) async-start(bf16[8,4096,512]{1,2,0:T(8,128)(2,1)} %reshape.346), calls=%async_computation | async-start | bytes 67108864 | tf_op jit(solution)/shard_map/all_to_all | solution.py:76
  212.2 793.9 %all-reduce.2.cloned.1.call-start = ((), (), s32[]{:S(2)}) async-start(), calls=%async_computation.1 | async-start | bytes 5242880 | tf_op jit(solution)/shard_map/psum | solution.py:12
  944.9 131.4 %all-gather.2.cloned.1.call-start = ((), (), s32[]{:S(2)}) async-start(), calls=%async_computation.2 | async-start | bytes 7864320 | tf_op jit(solution)/shard_map/all_gather | solution.py:100
  1006.1 92.7 %copy-start.1 = (bf16[5120,256]{1,0:T(8,128)(2,1)S(1)}, bf16[5120,256]{1,0:T(8,128)(2,1)}, u32[]{:S(2)}) copy-start(bf16[5120,256]{1,0:T(8,128)(2,1)} %all-reduce.2.cloned.1.call-done) | copy-start | bytes 7864324
Sparse Core Ops, SparseCore 0:
  945.0 61.0 all-reduce.1
  1007.7 68.6 all-gather.1
where the time goes:
time: 1110 us
  waiting for transfers between devices  492 us (44%)
  local copies, waits for them, and re-layouts  377 us (34%)
  matrix products  179 us (16%)
  other arithmetic  37.7 us (3%)
  between operations  14.2 us (1%)
    all_to_all x1, waiting for transfers between devices, local(): lax.all_to_all(outgoing, ('row', 'col'), split_axis=0, concat_axis=0, til...  361 us
    convert_element_type x1, local copies, waits for them, and re-layouts, local(): placed_cols = jnp.einsum('rsabec,rseq->rabqc', tiles, per_source, preferr...  109 us
    dot_general x2, matrix products, local(): jnp.einsum('ibjc,ipa,jqe->pqabec', tiles_four, row_pick, col_send, prefer...  83.1 us
    unnamed x10, local copies, waits for them, and re-layouts  83 us
    all_gather x1, waiting for transfers between devices, local(): all_panel = lax.all_gather(row_panel, 'row', axis=0, tiled=True)  70.2 us
    psum x1, waiting for transfers between devices, from_root(): return lax.psum(jnp.where(mine, shard, jnp.zeros_like(shard)), axis)  61.2 us
    reshape x1, local copies, waits for them, and re-layouts, local(): assembled.reshape(part_rows, part_cols) + front_orig.astype(jnp.float32)  52.2 us
    reshape x1, local copies, waits for them, and re-layouts, local(): outgoing = outgoing.reshape(n_row * n_col, row_cap * B, col_cap * B)  49.3 us
  transfers between devices with their start and end apart: 3, of which 3 were waited for; matrix products, arithmetic and copies ran while one was open for 0% of the time, Pallas kernels for 0%

commit v1 on v0

v1 whole, which is shorter than its diff:
```python
import functools

import jax
import jax.numpy as jnp
from jax import lax
from jax.experimental import pallas as pl
from jax.experimental.pallas import tpu as pltpu
from jax.sharding import PartitionSpec as P

B = 128
PANEL = 256
PANEL_BLOCKS = PANEL // B
VMEM_LIMIT = 48 * 1024 * 1024


def largest_group(count, limit):
    return max(g for g in range(1, limit + 1) if count % g == 0)


def rank_in_owner(ids, owners):
    same = owners[..., :, None] == owners[..., None, :]
    smaller = ids[..., None, :] < ids[..., :, None]
    return jnp.sum(same & smaller, axis=-1, dtype=jnp.int32)


def source_of_slot(ids, owner_width, capacity, owners_count):
    owners = ids // owner_width
    slots = owners * capacity + rank_in_owner(ids, owners)
    match = slots[None, :] == jnp.arange(owners_count * capacity, dtype=jnp.int32)[:, None]
    return jnp.sum(jnp.where(match, jnp.arange(ids.shape[0], dtype=jnp.int32)[None, :], 0), axis=1)


def pack_kernel(group, n_col, col_cap, first, width, row_src, col_src, *refs):
    out = refs[group]
    for c in range(n_col):
        for b in range(width):
            src = pl.multiple_of(col_src[c * col_cap + first + b] * B, B)
            for g in range(group):
                out[0, c, g * B:(g + 1) * B, b * B:(b + 1) * B] = refs[g][:, pl.ds(src, B)]


def pack(child, row_src, col_src, n_row, n_col, row_cap, col_cap, first, width):
    group = largest_group(row_cap, 4)
    steps = row_cap // group
    cols = child.shape[1]

    def row_map(g, r, s, row_src, col_src):
        return (row_src[r * row_cap + s * group + g], 0)

    out_shape = (n_row, n_col, row_cap * B, width * B)
    size = n_row * n_col * row_cap * width * B * B
    return pl.pallas_call(
        functools.partial(pack_kernel, group, n_col, col_cap, first, width),
        grid_spec=pltpu.PrefetchScalarGridSpec(
            num_scalar_prefetch=2,
            grid=(n_row, steps),
            in_specs=[pl.BlockSpec((B, cols), functools.partial(row_map, g)) for g in range(group)],
            out_specs=pl.BlockSpec(
                (1, n_col, group * B, width * B), lambda r, s, row_src, col_src: (r, 0, s, 0)
            ),
        ),
        out_shape=jax.ShapeDtypeStruct(out_shape, jnp.bfloat16),
        compiler_params=pltpu.CompilerParams(vmem_limit_bytes=VMEM_LIMIT),
        cost_estimate=pl.CostEstimate(
            flops=0, bytes_accessed=2 * child.size + 2 * size, transcendentals=0
        ),
    )(row_src, col_src, *([child] * group))


def add_tiles(acc, group, chunks, n_col, col_cap, has_row, col_to, tiles):
    step = pl.program_id(0)
    for g in range(group):
        for k in range(2):
            @pl.when(has_row[k, step * group + g] > 0)
            def _():
                for h, (first, width) in enumerate(chunks):
                    ref = tiles[(g * 2 + k) * len(chunks) + h]
                    for t in range(n_col):
                        for b in range(width):
                            at = pl.multiple_of(col_to[k, t * col_cap + first + b] * B, B)
                            acc[g * B:(g + 1) * B, pl.ds(at, B)] += ref[
                                0, t, :, b * B:(b + 1) * B
                            ].astype(jnp.float32)


def panel_kernel(group, chunks, n_col, col_cap, src, slot, has_row, col_to, *refs):
    front_ref, inverse_ref = refs[:2]
    tiles, out, acc = refs[2:-2], refs[-2], refs[-1]
    acc[:, :PANEL] = front_ref[...].astype(jnp.float32)
    add_tiles(acc, group, chunks, n_col, col_cap, has_row, col_to, tiles)
    out[...] = jnp.dot(
        acc[:, :PANEL].astype(jnp.bfloat16), inverse_ref[...], preferred_element_type=jnp.float32
    ).astype(jnp.bfloat16)


def schur_kernel(group, chunks, n_col, col_cap, strip, src, slot, has_row, col_to, *refs):
    front_ref, row_ref, col_ref = refs[:3]
    tiles, out, acc = refs[3:-2], refs[-2], refs[-1]
    width = front_ref.shape[1]
    acc[:, :width] = front_ref[...].astype(jnp.float32)
    add_tiles(acc, group, chunks, n_col, col_cap, has_row, col_to, tiles)
    for at in range(0, width, strip):
        update = lax.dot_general(
            row_ref[...], col_ref[at:at + strip, :], (((1,), (1,)), ((), ())),
            preferred_element_type=jnp.float32,
        )
        front = acc[:, at:at + strip].astype(jnp.bfloat16).astype(jnp.float32)
        out[:, at:at + strip] = (front - update).astype(jnp.bfloat16)


def gather_call(body, tables, front, extra, extra_specs, incoming, chunks, acc_cols, group, out_cols,
                front_cols, flops):
    rows = front.shape[0]
    specs, arrays = [], []

    def tile_map(g, k, s, src, slot, has_row, col_to):
        return (src[k, s * group + g], 0, slot[k, s * group + g], 0)

    for g in range(group):
        for k in range(2):
            for array in incoming:
                n_col, width = array.shape[1], array.shape[3]
                specs.append(pl.BlockSpec((1, n_col, B, width), functools.partial(tile_map, g, k)))
                arrays.append(array)
    moved = rows * (front_cols + out_cols) * 2 + sum(2 * a.size for a in incoming)
    return pl.pallas_call(
        body,
        grid_spec=pltpu.PrefetchScalarGridSpec(
            num_scalar_prefetch=4,
            grid=(rows // (group * B),),
            in_specs=[pl.BlockSpec((group * B, front_cols), lambda s, *_: (s, 0))]
            + extra_specs + specs,
            out_specs=pl.BlockSpec((group * B, out_cols), lambda s, *_: (s, 0)),
            scratch_shapes=[pltpu.VMEM((group * B, acc_cols), jnp.float32)],
        ),
        out_shape=jax.ShapeDtypeStruct((rows, out_cols), jnp.bfloat16),
        compiler_params=pltpu.CompilerParams(vmem_limit_bytes=VMEM_LIMIT),
        cost_estimate=pl.CostEstimate(flops=flops, bytes_accessed=moved, transcendentals=0),
    )(*tables, front, *extra, *arrays)


def local(front_orig, child_updates, child_map, panel_inverse):
    n_row = lax.axis_size("row")
    n_col = lax.axis_size("col")
    me_row = lax.axis_index("row")
    me_col = lax.axis_index("col")
    rows_local, cols_local = child_updates.shape
    part_rows, part_cols = front_orig.shape
    senders = n_row // 2
    blocks_row = rows_local // B
    blocks_col = cols_local // B
    fine_count = max(n_row, n_col)
    prb = part_rows // B
    pcb = part_cols // B
    row_cap = max(1, blocks_row // fine_count) * (fine_count // n_row)
    col_cap = max(1, blocks_col // fine_count) * (fine_count // n_col)

    my_map = lax.dynamic_index_in_dim(child_map, me_row // senders, 0, keepdims=False)
    row_ids = lax.dynamic_slice_in_dim(child_map.reshape(-1), me_row * blocks_row, blocks_row)
    col_ids = lax.dynamic_slice_in_dim(my_map, me_col * blocks_col, blocks_col)
    row_src = source_of_slot(row_ids, prb, row_cap, n_row)
    col_src = source_of_slot(col_ids, pcb, col_cap, n_col)

    by_row = child_map.reshape(n_row, blocks_row)
    row_rank = rank_in_owner(by_row, by_row // prb).reshape(2, -1)
    sender = jnp.broadcast_to(
        jnp.arange(n_row, dtype=jnp.int32)[:, None], by_row.shape
    ).reshape(2, -1)
    mine = me_row * prb + jnp.arange(prb, dtype=jnp.int32)
    match = by_row.reshape(2, 1, -1) == mine[None, :, None]
    src = jnp.sum(jnp.where(match, sender[:, None, :], 0), axis=2)
    slot = jnp.sum(jnp.where(match, row_rank[:, None, :], 0), axis=2)
    has_row = jnp.sum(match, axis=2, dtype=jnp.int32)

    by_col = child_map.reshape(2, n_col, blocks_col)
    col_owner = by_col // pcb
    col_rank = rank_in_owner(by_col, col_owner)
    match = (col_owner == me_col)[:, :, None, :] & (
        col_rank[:, :, None, :] == jnp.arange(col_cap, dtype=jnp.int32)[None, None, :, None]
    )
    col_to = pcb + jnp.sum(
        jnp.where(match, (by_col - me_col * pcb - pcb)[:, :, None, :], 0), axis=3
    ).reshape(2, n_col * col_cap)

    head = min(PANEL_BLOCKS, col_cap)
    chunks = [(0, head)] + ([(head, col_cap - head)] if col_cap > head else [])
    incoming = []
    for first, width in chunks:
        outgoing = pack(
            child_updates, row_src, col_src, n_row, n_col, row_cap, col_cap, first, width
        ).reshape(n_row * n_col, row_cap * B, width * B)
        arrived = lax.all_to_all(outgoing, ("row", "col"), split_axis=0, concat_axis=0, tiled=True)
        incoming.append(arrived.reshape(n_row, n_col, row_cap * B, width * B))

    group = largest_group(prb, 2)
    panel_to = jnp.minimum(col_to, PANEL_BLOCKS)
    local_panel = gather_call(
        functools.partial(panel_kernel, group, chunks[:1], n_col, col_cap),
        (src, slot, has_row, panel_to), front_orig, (panel_inverse,),
        [pl.BlockSpec((PANEL, PANEL), lambda s, *_: (0, 0))],
        incoming[:1], chunks[:1], PANEL + B, group, PANEL, PANEL,
        2 * part_rows * PANEL * PANEL,
    )
    masked = jnp.where(me_col == 0, local_panel, jnp.zeros_like(local_panel))
    row_panel = lax.psum(masked, "col")
    all_panel = lax.all_gather(row_panel, "row", axis=0, tiled=True)
    col_panel = lax.dynamic_slice_in_dim(all_panel, me_col * part_cols, part_cols, 0)
    strip = part_cols // largest_group(part_cols // PANEL, 5)
    schur = gather_call(
        functools.partial(schur_kernel, group, chunks, n_col, col_cap, strip),
        (src, slot, has_row, col_to), front_orig, (row_panel, col_panel),
        [
            pl.BlockSpec((group * B, PANEL), lambda s, *_: (s, 0)),
            pl.BlockSpec((part_cols, PANEL), lambda s, *_: (0, 0)),
        ],
        incoming, chunks, part_cols + B, group, part_cols, part_cols,
        2 * part_rows * part_cols * PANEL,
    )
    return (schur, row_panel)


def solution(mesh):
    in_specs = (P(("hyp", "row"), "col"), P(("hyp", "row"), "col"), P("hyp", None), P("hyp", None))
    out_specs = (P(("hyp", "row"), "col"), P(("hyp", "row"), None))
    return jax.shard_map(local, mesh=mesh, in_specs=in_specs, out_specs=out_specs, check_vma=False)
```

time: 1110 us -> 553 us (0.50)
  local copies, waits for them, and re-layouts: 377 us -> 6.2 us
  matrix products: 179 us -> 0 us
  Pallas kernels: 0 us -> 103 us
  waiting for transfers between devices: 492 us -> 412 us
  other arithmetic: 37.7 us -> 4.17 us
    all_to_all x1 -> x2, waiting for transfers between devices: 361 us -> 161 us  [local(): lax.all_to_all(outgoing, ('row', 'col'), split_axis=0, concat_axis=0, til...]
    dot_general x6 -> x0, matrix products: 179 us -> none  [the longest x2 83.1 us: local(): jnp.einsum('ibjc,ipa,jqe->pqabec', tiles_four, row_pick, col_send, prefer...]
    convert_element_type x2 -> x0, local copies, waits for them, and re-layouts: 150 us -> none  [the longest x1 109 us: local(): placed_cols = jnp.einsum('rsabec,rseq->rabqc', tiles, per_source, preferr...]
    reshape x4 -> x2, local copies, waits for them, and re-layouts: 144 us -> 0.84 us  [the longest x1 0.76 us: local(): child_map.reshape(-1)]
    psum x1, waiting for transfers between devices: 61.2 us -> 181 us  [local(): row_panel = lax.psum(masked, 'col')]
    pallas_call x0 -> x4, Pallas kernels: none -> 103 us  [the longest x2 58.3 us: gather_call(): pl.pallas_call(body, grid_spec=pltpu.PrefetchScalarGridSpec(num_scalar_pr...]
    unnamed x10 -> x9, local copies, waits for them, and re-layouts: 83 us -> 2.82 us
    convert_element_type x3 -> x0, other arithmetic: 34.2 us -> none  [the longest x1 34.2 us: local(): front = front32.astype(jnp.bfloat16)]
  transfers between devices with their start and end apart: 3 -> 4, of which waited for: 3 -> 3; matrix products, arithmetic and copies ran while one was open for 0% -> 1% of each run, Pallas kernels for 0% -> 8%
where the time goes in v1:
time: 553 us; the launch traced here: 552 us
  waiting for transfers between devices  412 us (75%)
  Pallas kernels  103 us (19%)
  between operations  14.2 us (3%)
  starting transfers between devices  11.7 us (2%)
  local copies, waits for them, and re-layouts  6.2 us (1%)
    psum x1, waiting for transfers between devices, local(): row_panel = lax.psum(masked, 'col')  181 us
    all_to_all x2, waiting for transfers between devices, local(): lax.all_to_all(outgoing, ('row', 'col'), split_axis=0, concat_axis=0, til...  161 us
    all_gather x1, waiting for transfers between devices, local(): all_panel = lax.all_gather(row_panel, 'row', axis=0, tiled=True)  70.2 us
    pallas_call x2, Pallas kernels, gather_call(): pl.pallas_call(body, grid_spec=pltpu.PrefetchScalarGridSpec(num_scalar_pr...  58.3 us
    pallas_call x2, Pallas kernels, pack(): pl.pallas_call(functools.partial(pack_kernel, group, n_col, col_cap, firs...  44.9 us
    all_to_all x2, starting transfers between devices, local(): lax.all_to_all(outgoing, ('row', 'col'), split_axis=0, concat_axis=0, til...  11.6 us
  transfers between devices with their start and end apart: 4, of which 3 were waited for; matrix products, arithmetic and copies ran while one was open for 1% of the time, Pallas kernels for 8%

profile of v1, /device:TPU:0, one launch (start us, length us, event | category | flops | bytes accessed | tf_op | source)
XLA Modules:
  0.0 551.8 jit_solution(1964649545790406093)
XLA Ops:
  7.2 0.8 reshape.119
  7.9 0.8 and_select_fusion
  8.7 0.2 convert_reduce_fusion.3
  8.9 0.1 select_reduce_fusion.2.col_src
  9.0 0.1 and_select_fusion.2
  9.1 0.2 convert_reduce_fusion.2
  9.3 0.1 select_reduce_fusion.row_src
  9.4 22.5 %shard_map.59 = bf16[2,4,4096,256]{3,2,1,0:T(8,128)(2,1)} custom-call(s32[64]{0:T(128)S(1)} %select_reduce_fusion.row_src, s32[16]{0:T(128)S(1)} %select_reduce_fusion.2.col_src, bf16[8192,2048]{1,0:T(8,128)(2,1)} %refs_3_.3, bf16[8192,2048]{1,0:T(8,128)(2,1)} %refs_3_.3, bf16[8192,2048]{1,0:T(8,128)(2,1)} %refs_3_.3, bf16[8192,2048]{1,0:T(8,128)(2,1)} %refs_3_.3), custom_call_target="tpu_custom_call" | custom-call | bytes 50331648 | tf_op jit(solution)/shard_map/pallas_call | solution.py:52
  31.9 5.8 %all-to-all-start = ((bf16[8,4096,256]{2,1,0:T(8,128)(2,1)}), bf16[8,4096,256]{2,1,0:T(8,128)(2,1)}, u32[]{:S(2)}, u32[]{:S(2)}) async-start(bf16[8,4096,256]{2,1,0:T(8,128)(2,1)} %bitcast.15), calls=%async_computation | async-start | bytes 33554432 | tf_op jit(solution)/shard_map/all_to_all | solution.py:192
  37.7 22.4 %shard_map.61 = bf16[2,4,4096,256]{3,2,1,0:T(8,128)(2,1)} custom-call(s32[64]{0:T(128)S(1)} %select_reduce_fusion.row_src, s32[16]{0:T(128)S(1)} %select_reduce_fusion.2.col_src, bf16[8192,2048]{1,0:T(8,128)(2,1)} %refs_3_.3, bf16[8192,2048]{1,0:T(8,128)(2,1)} %refs_3_.3, bf16[8192,2048]{1,0:T(8,128)(2,1)} %refs_3_.3, bf16[8192,2048]{1,0:T(8,128)(2,1)} %refs_3_.3), custom_call_target="tpu_custom_call" | custom-call | bytes 50331648 | tf_op jit(solution)/shard_map/pallas_call | solution.py:52
  60.1 161.2 %all-to-all-done = bf16[8,4096,256]{2,1,0:T(8,128)(2,1)} async-done(((bf16[8,4096,256]{2,1,0:T(8,128)(2,1)}), bf16[8,4096,256]{2,1,0:T(8,128)(2,1)}, u32[]{:S(2)}, u32[]{:S(2)}) %all-to-all-start) | async-done | bytes 16777248 | tf_op jit(solution)/shard_map/all_to_all | solution.py:192
  221.3 5.9 %all-to-all-start.1 = ((bf16[8,4096,256]{2,1,0:T(8,128)(2,1)}), bf16[8,4096,256]{2,1,0:T(8,128)(2,1)}, u32[]{:S(2)}, u32[]{:S(2)}) async-start(bf16[8,4096,256]{2,1,0:T(8,128)(2,1)} %bitcast.14), calls=%async_computation.1 | async-start | bytes 33554432 | tf_op jit(solution)/shard_map/all_to_all | solution.py:192
  227.2 0.0 all-reduce.2.cloned.1.call-start
  227.2 0.0 copy-done.3
  227.2 0.1 reshape.118
  227.4 0.3 convert_reduce_fusion
  227.7 0.2 select_reduce_fusion.1
  227.9 0.1 add.73.col_to
  228.0 0.2 convert_reduce_fusion.1
  228.2 0.3 fusion.2
  228.5 18.9 %shard_map.60 = bf16[5120,256]{1,0:T(8,128)(2,1)S(1)} custom-call(s32[2,40]{1,0:T(2,128)S(1)} %get-tuple-element.4.src, s32[2,40]{1,0:T(2,128)S(1)} %get-tuple-element.3.slot, s32[2,40]{1,0:T(2,128)S(1)} %get-tuple-element.2.has_row, s32[2,16]{1,0:T(2,128)S(1)} %broadcast_minimum_fusion.col_to, bf16[5120,2560]{1,0:T(8,128)(2,1)} %refs_0_.7, ...), custom_call_target="tpu_custom_call" | custom-call | flops 671088640 | bytes 22020096 | tf_op jit(solution)/shard_map/pallas_call | solution.py:126
  247.4 1.7 broadcast_select_fusion
  249.1 0.0 all-reduce.2.cloned.1.call-update
  249.1 0.0 all-gather.2.cloned.1.call-start
  249.2 180.9 %all-reduce.2.cloned.1.call-done.refs_1_ = bf16[5120,256]{1,0:T(8,128)(2,1)} async-done(((bf16[5120,256]{1,0:T(8,128)(2,1)}), bf16[5120,256]{1,0:T(8,128)(2,1)}) %all-reduce.2.cloned.1.call-update) | async-done | bytes 2621456 | tf_op jit(solution)/shard_map/psum | solution.py:205
  430.1 0.0 all-gather.2.cloned.1.call-update
  430.1 70.2 %all-gather.2.cloned.1.call-done = bf16[10240,256]{1,0:T(8,128)(2,1)} async-done(((bf16[5120,256]{1,0:T(8,128)(2,1)}), bf16[10240,256]{1,0:T(8,128)(2,1)}) %all-gather.2.cloned.1.call-update) | async-done | bytes 5242896 | tf_op jit(solution)/shard_map/all_gather | solution.py:206
  500.3 2.5 constant_dynamic-slice_fusion.refs_2_
  502.8 0.0 all-to-all-done.1
  502.8 1.3 copy-done.1
  504.1 39.4 %shard_map.62 = bf16[5120,2560]{1,0:T(8,128)(2,1)} custom-call(s32[2,40]{1,0:T(2,128)S(1)} %get-tuple-element.4.src, s32[2,40]{1,0:T(2,128)S(1)} %get-tuple-element.3.slot, s32[2,40]{1,0:T(2,128)S(1)} %get-tuple-element.2.has_row, s32[2,16]{1,0:T(2,128)S(1)} %add.73.col_to, bf16[5120,2560]{1,0:T(8,128)(2,1)} %refs_0_.7, bf16[5120,256]{1,0:T(8,128)(2,1)S(1)} %copy-done, ...), custom_call_target="tpu_custom_call" | custom-call | flops 6710886400 | bytes 85983232 | tf_op jit(solution)/shard_map/pallas_call | solution.py:126
  543.5 1.5 copy.7
  (15 shorter events, 0.1 us)
Async XLA Ops:
  31.9 189.4 %all-to-all-start = ((bf16[8,4096,256]{2,1,0:T(8,128)(2,1)}), bf16[8,4096,256]{2,1,0:T(8,128)(2,1)}, u32[]{:S(2)}, u32[]{:S(2)}) async-start(bf16[8,4096,256]{2,1,0:T(8,128)(2,1)} %bitcast.15), calls=%async_computation | async-start | bytes 33554432 | tf_op jit(solution)/shard_map/all_to_all | solution.py:192
  221.3 6.0 %copy-start.3 = (s32[2,64]{1,0:T(2,128)S(1)}, s32[2,64]{1,0:T(2,128)}, u32[]{:S(2)}) copy-start(s32[2,64]{1,0:T(2,128)} %param.6) | copy-start | bytes 1540
  221.3 7.2 %copy-start.2 = (bf16[256,256]{1,0:T(8,128)(2,1)S(1)}, bf16[256,256]{1,0:T(8,128)(2,1)}, u32[]{:S(2)}) copy-start(bf16[256,256]{1,0:T(8,128)(2,1)} %refs_1_.4) | copy-start | bytes 393220
  221.3 281.5 %all-to-all-start.1 = ((bf16[8,4096,256]{2,1,0:T(8,128)(2,1)}), bf16[8,4096,256]{2,1,0:T(8,128)(2,1)}, u32[]{:S(2)}, u32[]{:S(2)}) async-start(bf16[8,4096,256]{2,1,0:T(8,128)(2,1)} %bitcast.14), calls=%async_computation.1 | async-start | bytes 33554432 | tf_op jit(solution)/shard_map/all_to_all | solution.py:192
  227.2 202.9 %all-reduce.2.cloned.1.call-start = ((), (), s32[]{:S(2)}) async-start(), calls=%async_computation.2 | async-start | bytes 5242880 | tf_op jit(solution)/shard_map/psum | solution.py:205
  249.1 251.2 %all-gather.2.cloned.1.call-start = ((), (), s32[]{:S(2)}) async-start(), calls=%async_computation.3 | async-start | bytes 7864320 | tf_op jit(solution)/shard_map/all_gather | solution.py:206
  430.1 72.7 %copy-start = (bf16[5120,256]{1,0:T(8,128)(2,1)S(1)}, bf16[5120,256]{1,0:T(8,128)(2,1)}, u32[]{:S(2)}) copy-start(bf16[5120,256]{1,0:T(8,128)(2,1)} %all-reduce.2.cloned.1.call-done.refs_1_) | copy-start | bytes 7864324
  502.8 1.3 copy-start.1
Sparse Core Ops, SparseCore 0:
  249.2 180.8 all-reduce.1
  431.7 68.6 all-gather.1

commit v2 on v1

--- a/solution.py
+++ b/solution.py
@@ -139,6 +139,51 @@
     )(*tables, front, *extra, *arrays)
 
 
+def spread(value, pairs, receives):
+    got = lax.ppermute(value, ("row", "col"), pairs)
+    return jnp.where(receives, got, value)
+
+
+def share_panel(panel, part_cols):
+    n_row, n_col = lax.axis_size("row"), lax.axis_size("col")
+    me_row, me_col = lax.axis_index("row"), lax.axis_index("col")
+    part_rows = panel.shape[0]
+    one_owner = part_rows % part_cols == 0
+    groups = part_rows // part_cols if one_owner else 1
+    count = 2 * groups
+    pieces = jnp.split(panel, count, axis=0)
+    reach = n_col
+    while reach > 1:
+        half = reach // 2
+        pairs = [
+            (r * n_col + c, r * n_col + c + half) for r in range(n_row) for c in range(0, n_col, reach)
+        ]
+        pieces = [spread(piece, pairs, me_col % reach == half) for piece in pieces]
+        reach = half
+    row_panel = jnp.concatenate(pieces, axis=0)
+    if not one_owner:
+        all_panel = lax.all_gather(row_panel, "row", axis=0, tiled=True)
+        return row_panel, lax.dynamic_slice_in_dim(all_panel, me_col * part_cols, part_cols, 0)
+    matching = []
+    for k in range(2):
+        piece = pieces[k]
+        for g in range(1, groups):
+            piece = jnp.where(me_col % groups == g, pieces[2 * g + k], piece)
+        matching.append(piece)
+    away = (me_row - me_col // groups + n_row) % n_row
+    reach = n_row
+    while reach > 1:
+        half = reach // 2
+        pairs = []
+        for c in range(n_col):
+            for i in range(0, n_row, reach):
+                sender, receiver = (c // groups + i) % n_row, (c // groups + i + half) % n_row
+                pairs.append((sender * n_col + c, receiver * n_col + c))
+        matching = [spread(piece, pairs, away % reach == half) for piece in matching]
+        reach = half
+    return row_panel, jnp.concatenate(matching, axis=0)
+
+
 def local(front_orig, child_updates, child_map, panel_inverse):
     n_row = lax.axis_size("row")
     n_col = lax.axis_size("col")
@@ -201,10 +246,7 @@
         incoming[:1], chunks[:1], PANEL + B, group, PANEL, PANEL,
         2 * part_rows * PANEL * PANEL,
     )
-    masked = jnp.where(me_col == 0, local_panel, jnp.zeros_like(local_panel))
-    row_panel = lax.psum(masked, "col")
-    all_panel = lax.all_gather(row_panel, "row", axis=0, tiled=True)
-    col_panel = lax.dynamic_slice_in_dim(all_panel, me_col * part_cols, part_cols, 0)
+    row_panel, col_panel = share_panel(local_panel, part_cols)
     strip = part_cols // largest_group(part_cols // PANEL, 5)
     schur = gather_call(
         functools.partial(schur_kernel, group, chunks, n_col, col_cap, strip),

time: 553 us -> 519 us (0.939)
  waiting for transfers between devices: 412 us -> 366 us
  starting transfers between devices: 11.7 us -> 34.8 us
  between operations: 14.2 us -> 0.93 us
    ppermute x0 -> x10, waiting for transfers between devices: none -> 205 us  [spread(): got = lax.ppermute(value, ('row', 'col'), pairs)]
    psum x1 -> x0, waiting for transfers between devices: 181 us -> none  [local(): row_panel = lax.psum(masked, 'col')]
    all_gather x1 -> x0, waiting for transfers between devices: 70.2 us -> none  [local(): all_panel = lax.all_gather(row_panel, 'row', axis=0, tiled=True)]
    ppermute x0 -> x10, starting transfers between devices: none -> 23.2 us  [spread(): got = lax.ppermute(value, ('row', 'col'), pairs)]
  transfers between devices with their start and end apart: 4 -> 12, of which waited for: 3 -> 7; matrix products, arithmetic and copies ran while one was open for 1% -> 1% of each run, Pallas kernels for 8% -> 8%
where the time goes in v2:
time: 519 us; the launch traced here: 518 us
  waiting for transfers between devices  366 us (71%)
  Pallas kernels  105 us (20%)
  starting transfers between devices  34.8 us (7%)
  other arithmetic  8.6 us (2%)
    ppermute x10, waiting for transfers between devices, spread(): got = lax.ppermute(value, ('row', 'col'), pairs)  205 us
    all_to_all x2, waiting for transfers between devices, local(): lax.all_to_all(outgoing, ('row', 'col'), split_axis=0, concat_axis=0, til...  161 us
    pallas_call x2, Pallas kernels, gather_call(): pl.pallas_call(body, grid_spec=pltpu.PrefetchScalarGridSpec(num_scalar_pr...  59.7 us
    pallas_call x2, Pallas kernels, pack(): pl.pallas_call(functools.partial(pack_kernel, group, n_col, col_cap, firs...  45 us
    ppermute x10, starting transfers between devices, spread(): got = lax.ppermute(value, ('row', 'col'), pairs)  23.2 us
    all_to_all x2, starting transfers between devices, local(): lax.all_to_all(outgoing, ('row', 'col'), split_axis=0, concat_axis=0, til...  11.6 us
  transfers between devices with their start and end apart: 12, of which 7 were waited for; matrix products, arithmetic and copies ran while one was open for 1% of the time, Pallas kernels for 8%

profile of v2, /device:TPU:0, one launch (start us, length us, event | category | flops | bytes accessed | tf_op | source)
XLA Modules:
  0.0 517.7 jit_solution(5238829528435425755)
XLA Ops:
  0.6 0.8 reshape.119
  1.4 0.8 and_select_fusion
  2.9 22.5 %shard_map.59 = bf16[2,4,4096,256]{3,2,1,0:T(8,128)(2,1)} custom-call(s32[64]{0:T(128)S(1)} %select_reduce_fusion.row_src, s32[16]{0:T(128)S(1)} %select_reduce_fusion.2.col_src, bf16[8192,2048]{1,0:T(8,128)(2,1)} %refs_3_.3, bf16[8192,2048]{1,0:T(8,128)(2,1)} %refs_3_.3, bf16[8192,2048]{1,0:T(8,128)(2,1)} %refs_3_.3, bf16[8192,2048]{1,0:T(8,128)(2,1)} %refs_3_.3), custom_call_target="tpu_custom_call" | custom-call | bytes 50331648 | tf_op jit(solution)/shard_map/pallas_call | solution.py:52
  25.4 5.8 %all-to-all-start = ((bf16[8,4096,256]{2,1,0:T(8,128)(2,1)}), bf16[8,4096,256]{2,1,0:T(8,128)(2,1)}, u32[]{:S(2)}, u32[]{:S(2)}) async-start(bf16[8,4096,256]{2,1,0:T(8,128)(2,1)} %bitcast.15), calls=%async_computation | async-start | bytes 33554432 | tf_op jit(solution)/shard_map/all_to_all | solution.py:237
  31.2 22.5 %shard_map.61 = bf16[2,4,4096,256]{3,2,1,0:T(8,128)(2,1)} custom-call(s32[64]{0:T(128)S(1)} %select_reduce_fusion.row_src, s32[16]{0:T(128)S(1)} %select_reduce_fusion.2.col_src, bf16[8192,2048]{1,0:T(8,128)(2,1)} %refs_3_.3, bf16[8192,2048]{1,0:T(8,128)(2,1)} %refs_3_.3, bf16[8192,2048]{1,0:T(8,128)(2,1)} %refs_3_.3, bf16[8192,2048]{1,0:T(8,128)(2,1)} %refs_3_.3), custom_call_target="tpu_custom_call" | custom-call | bytes 50331648 | tf_op jit(solution)/shard_map/pallas_call | solution.py:52
  53.7 161.1 %all-to-all-done = bf16[8,4096,256]{2,1,0:T(8,128)(2,1)} async-done(((bf16[8,4096,256]{2,1,0:T(8,128)(2,1)}), bf16[8,4096,256]{2,1,0:T(8,128)(2,1)}, u32[]{:S(2)}, u32[]{:S(2)}) %all-to-all-start) | async-done | bytes 16777248 | tf_op jit(solution)/shard_map/all_to_all | solution.py:237
  214.7 5.9 %all-to-all-start.1 = ((bf16[8,4096,256]{2,1,0:T(8,128)(2,1)}), bf16[8,4096,256]{2,1,0:T(8,128)(2,1)}, u32[]{:S(2)}, u32[]{:S(2)}) async-start(bf16[8,4096,256]{2,1,0:T(8,128)(2,1)} %bitcast.14), calls=%async_computation.1 | async-start | bytes 33554432 | tf_op jit(solution)/shard_map/all_to_all | solution.py:237
  220.7 0.3 convert_reduce_fusion
  221.9 19.1 %shard_map.60 = bf16[5120,256]{1,0:T(8,128)(2,1)S(1)} custom-call(s32[2,40]{1,0:T(2,128)S(1)} %get-tuple-element.4.src, s32[2,40]{1,0:T(2,128)S(1)} %get-tuple-element.3.slot, s32[2,40]{1,0:T(2,128)S(1)} %get-tuple-element.2.has_row, s32[2,16]{1,0:T(2,128)S(1)} %broadcast_minimum_fusion.col_to, bf16[5120,2560]{1,0:T(8,128)(2,1)} %refs_0_.7, ...), custom_call_target="tpu_custom_call" | custom-call | flops 671088640 | bytes 22020096 | tf_op jit(solution)/shard_map/pallas_call | solution.py:126
  241.0 4.6 collective-permute-start.4
  245.6 162.8 %collective-permute-done.4 = bf16[1280,256]{1,0:T(8,128)(2,1)} collective-permute-done((bf16[1280,256]{1,0:T(8,128)(2,1)S(1)}, bf16[1280,256]{1,0:T(8,128)(2,1)}, u32[]{:S(2)}, u32[]{:S(2)}) %collective-permute-start.4) | collective-permute-done | bytes 655392 | tf_op jit(solution)/shard_map/ppermute | solution.py:143
  408.6 5.6 %collective-permute-start.6 = (bf16[1280,256]{1,0:T(8,128)(2,1)S(1)}, bf16[1280,256]{1,0:T(8,128)(2,1)S(1)}, u32[]{:S(2)}, u32[]{:S(2)}) collective-permute-start(bf16[1280,256]{1,0:T(8,128)(2,1)S(1)} %get-tuple-element.18), channel_id=1, source_target_pairs={{0,2},{4,6},{8,10},{12,14},{16,18},{20,22},{24,26},{28,30}} | collective-permute-start | bytes 1966088 | tf_op jit(solution)/shard_map/ppermute | solution.py:143
  414.2 1.3 collective-permute-start.2
  415.5 1.3 collective-permute-start
  416.9 5.4 %collective-permute-done.6 = bf16[1280,256]{1,0:T(8,128)(2,1)S(1)} collective-permute-done((bf16[1280,256]{1,0:T(8,128)(2,1)S(1)}, bf16[1280,256]{1,0:T(8,128)(2,1)S(1)}, u32[]{:S(2)}, u32[]{:S(2)}) %collective-permute-start.6) | collective-permute-done | bytes 655392 | tf_op jit(solution)/shard_map/ppermute | solution.py:143
  422.2 7.0 %collective-permute-done.2 = bf16[1280,256]{1,0:T(8,128)(2,1)S(1)} collective-permute-done((bf16[1280,256]{1,0:T(8,128)(2,1)S(1)}, bf16[1280,256]{1,0:T(8,128)(2,1)S(1)}, u32[]{:S(2)}, u32[]{:S(2)}) %collective-permute-start.2) | collective-permute-done | bytes 655392 | tf_op jit(solution)/shard_map/ppermute | solution.py:143
  429.3 7.0 %collective-permute-done = bf16[1280,256]{1,0:T(8,128)(2,1)S(1)} collective-permute-done((bf16[1280,256]{1,0:T(8,128)(2,1)S(1)}, bf16[1280,256]{1,0:T(8,128)(2,1)S(1)}, u32[]{:S(2)}, u32[]{:S(2)}) %collective-permute-start) | collective-permute-done | bytes 655392 | tf_op jit(solution)/shard_map/ppermute | solution.py:143
  436.3 1.4 broadcast_select_fusion.5
  437.7 1.3 collective-permute-start.3
  439.0 1.3 collective-permute-start.7
  440.4 1.3 collective-permute-start.5
  441.7 1.3 collective-permute-start.1
  443.1 1.4 broadcast_select_fusion.6
  444.6 3.6 collective-permute-start.9
  448.2 1.3 broadcast_select_fusion.7
  449.5 1.3 collective-permute-start.8
  450.8 0.5 pad_maximum_fusion.refs_1_
  451.4 12.0 %collective-permute-done.9 = bf16[1280,256]{1,0:T(8,128)(2,1)S(1)} collective-permute-done((bf16[1280,256]{1,0:T(8,128)(2,1)S(1)}, bf16[1280,256]{1,0:T(8,128)(2,1)S(1)}, u32[]{:S(2)}, u32[]{:S(2)}) %collective-permute-start.9) | collective-permute-done | bytes 655392 | tf_op jit(solution)/shard_map/ppermute | solution.py:143
  463.4 11.1 %collective-permute-done.8 = bf16[1280,256]{1,0:T(8,128)(2,1)S(1)} collective-permute-done((bf16[1280,256]{1,0:T(8,128)(2,1)S(1)}, bf16[1280,256]{1,0:T(8,128)(2,1)S(1)}, u32[]{:S(2)}, u32[]{:S(2)}) %collective-permute-start.8) | collective-permute-done | bytes 655392 | tf_op jit(solution)/shard_map/ppermute | solution.py:143
  474.6 1.1 pad_maximum_fusion.1.refs_2_
  475.8 1.3 copy-done.1
  477.1 40.6 %shard_map.62 = bf16[5120,2560]{1,0:T(8,128)(2,1)} custom-call(s32[2,40]{1,0:T(2,128)S(1)} %get-tuple-element.4.src, s32[2,40]{1,0:T(2,128)S(1)} %get-tuple-element.3.slot, s32[2,40]{1,0:T(2,128)S(1)} %get-tuple-element.2.has_row, s32[2,16]{1,0:T(2,128)S(1)} %add.94.col_to, bf16[5120,2560]{1,0:T(8,128)(2,1)} %refs_0_.7, ...), custom_call_target="tpu_custom_call" | custom-call | flops 6710886400 | bytes 85983232 | tf_op jit(solution)/shard_map/pallas_call | solution.py:126
  (35 shorter events, 2.0 us)
Async XLA Ops:
  25.4 189.3 %all-to-all-start = ((bf16[8,4096,256]{2,1,0:T(8,128)(2,1)}), bf16[8,4096,256]{2,1,0:T(8,128)(2,1)}, u32[]{:S(2)}, u32[]{:S(2)}) async-start(bf16[8,4096,256]{2,1,0:T(8,128)(2,1)} %bitcast.15), calls=%async_computation | async-start | bytes 33554432 | tf_op jit(solution)/shard_map/all_to_all | solution.py:237
  214.7 5.9 %copy-start.3 = (s32[2,64]{1,0:T(2,128)S(1)}, s32[2,64]{1,0:T(2,128)}, u32[]{:S(2)}) copy-start(s32[2,64]{1,0:T(2,128)} %param.6) | copy-start | bytes 1540
  214.7 7.1 %copy-start.2 = (bf16[256,256]{1,0:T(8,128)(2,1)S(1)}, bf16[256,256]{1,0:T(8,128)(2,1)}, u32[]{:S(2)}) copy-start(bf16[256,256]{1,0:T(8,128)(2,1)} %refs_1_.4) | copy-start | bytes 393220
  214.7 261.1 %all-to-all-start.1 = ((bf16[8,4096,256]{2,1,0:T(8,128)(2,1)}), bf16[8,4096,256]{2,1,0:T(8,128)(2,1)}, u32[]{:S(2)}, u32[]{:S(2)}) async-start(bf16[8,4096,256]{2,1,0:T(8,128)(2,1)} %bitcast.14), calls=%async_computation.1 | async-start | bytes 33554432 | tf_op jit(solution)/shard_map/all_to_all | solution.py:237
  241.0 167.4 %collective-permute-start.4 = (bf16[1280,256]{1,0:T(8,128)(2,1)S(1)}, bf16[1280,256]{1,0:T(8,128)(2,1)}, u32[]{:S(2)}, u32[]{:S(2)}) collective-permute-start(bf16[1280,256]{1,0:T(8,128)(2,1)S(1)} %split.18), channel_id=1, source_target_pairs={{0,2},{4,6},{8,10},{12,14},{16,18},{20,22},{24,26},{28,30}} | collective-permute-start | bytes 1966088 | tf_op jit(solution)/shard_map/ppermute | solution.py:143
  408.6 13.7 %collective-permute-start.6 = (bf16[1280,256]{1,0:T(8,128)(2,1)S(1)}, bf16[1280,256]{1,0:T(8,128)(2,1)S(1)}, u32[]{:S(2)}, u32[]{:S(2)}) collective-permute-start(bf16[1280,256]{1,0:T(8,128)(2,1)S(1)} %get-tuple-element.18), channel_id=1, source_target_pairs={{0,2},{4,6},{8,10},{12,14},{16,18},{20,22},{24,26},{28,30}} | collective-permute-start | bytes 1966088 | tf_op jit(solution)/shard_map/ppermute | solution.py:143
  414.2 15.1 %collective-permute-start.2 = (bf16[1280,256]{1,0:T(8,128)(2,1)S(1)}, bf16[1280,256]{1,0:T(8,128)(2,1)S(1)}, u32[]{:S(2)}, u32[]{:S(2)}) collective-permute-start(bf16[1280,256]{1,0:T(8,128)(2,1)S(1)} %get-tuple-element.19), channel_id=1, source_target_pairs={{0,2},{4,6},{8,10},{12,14},{16,18},{20,22},{24,26},{28,30}} | collective-permute-start | bytes 1966088 | tf_op jit(solution)/shard_map/ppermute | solution.py:143
  415.5 20.8 %collective-permute-start = (bf16[1280,256]{1,0:T(8,128)(2,1)S(1)}, bf16[1280,256]{1,0:T(8,128)(2,1)S(1)}, u32[]{:S(2)}, u32[]{:S(2)}) collective-permute-start(bf16[1280,256]{1,0:T(8,128)(2,1)S(1)} %get-tuple-element.20), channel_id=1, source_target_pairs={{0,2},{4,6},{8,10},{12,14},{16,18},{20,22},{24,26},{28,30}} | collective-permute-start | bytes 1966088 | tf_op jit(solution)/shard_map/ppermute | solution.py:143
  437.7 5.4 %collective-permute-start.3 = (bf16[1280,256]{1,0:T(8,128)(2,1)}, bf16[1280,256]{1,0:T(8,128)(2,1)S(1)}, u32[]{:S(2)}, u32[]{:S(2)}) collective-permute-start(bf16[1280,256]{1,0:T(8,128)(2,1)} %get-tuple-element.22), channel_id=1, source_target_pairs={{0,1},{2,3},{4,5},{6,7},{8,9},{10,11},{12,13},{14,15},{16,17},{18,... | collective-permute-start | bytes 1966088 | tf_op jit(solution)/shard_map/ppermute | solution.py:143
  439.0 4.1 collective-permute-start.7
  440.4 7.8 %collective-permute-start.5 = (bf16[1280,256]{1,0:T(8,128)(2,1)S(1)}, bf16[1280,256]{1,0:T(8,128)(2,1)S(1)}, u32[]{:S(2)}, u32[]{:S(2)}) collective-permute-start(bf16[1280,256]{1,0:T(8,128)(2,1)S(1)} %get-tuple-element.17), channel_id=1, source_target_pairs={{0,1},{2,3},{4,5},{6,7},{8,9},{10,11},{12,13},{14,15},{16,17},{18,... | collective-permute-start | bytes 1966088 | tf_op jit(solution)/shard_map/ppermute | solution.py:143
  441.7 6.5 %collective-permute-start.1 = (bf16[1280,256]{1,0:T(8,128)(2,1)}, bf16[1280,256]{1,0:T(8,128)(2,1)S(1)}, u32[]{:S(2)}, u32[]{:S(2)}) collective-permute-start(bf16[1280,256]{1,0:T(8,128)(2,1)} %get-tuple-element.21), channel_id=1, source_target_pairs={{0,1},{2,3},{4,5},{6,7},{8,9},{10,11},{12,13},{14,15},{16,17},{18,... | collective-permute-start | bytes 1966088 | tf_op jit(solution)/shard_map/ppermute | solution.py:143
  444.6 18.8 %collective-permute-start.9 = (bf16[1280,256]{1,0:T(8,128)(2,1)S(1)}, bf16[1280,256]{1,0:T(8,128)(2,1)S(1)}, u32[]{:S(2)}, u32[]{:S(2)}) collective-permute-start(bf16[1280,256]{1,0:T(8,128)(2,1)S(1)} %get-tuple-element.8), channel_id=1, source_target_pairs={{0,4},{1,5},{6,2},{7,3},{8,12},{9,13},{14,10},{15,11},{16,20},{17,... | collective-permute-start | bytes 1966088 | tf_op jit(solution)/shard_map/ppermute | solution.py:143
  449.5 25.0 %collective-permute-start.8 = (bf16[1280,256]{1,0:T(8,128)(2,1)S(1)}, bf16[1280,256]{1,0:T(8,128)(2,1)S(1)}, u32[]{:S(2)}, u32[]{:S(2)}) collective-permute-start(bf16[1280,256]{1,0:T(8,128)(2,1)S(1)} %get-tuple-element.5), channel_id=1, source_target_pairs={{0,4},{1,5},{6,2},{7,3},{8,12},{9,13},{14,10},{15,11},{16,20},{17,... | collective-permute-start | bytes 1966088 | tf_op jit(solution)/shard_map/ppermute | solution.py:143
  451.4 24.4 %copy-start = (bf16[5120,256]{1,0:T(8,128)(2,1)}, bf16[5120,256]{1,0:T(8,128)(2,1)S(1)}, u32[]{:S(2)}) copy-start(bf16[5120,256]{1,0:T(8,128)(2,1)S(1)} %pad_maximum_fusion.refs_1_) | copy-start | bytes 7864324
  475.8 1.3 copy-start.1

commit v3 on v2

--- a/solution.py
+++ b/solution.py
@@ -40,7 +40,7 @@
 
 
 def pack(child, row_src, col_src, n_row, n_col, row_cap, col_cap, first, width):
-    group = largest_group(row_cap, 4)
+    group = largest_group(row_cap, 8)
     steps = row_cap // group
     cols = child.shape[1]
 
@@ -139,9 +139,8 @@
     )(*tables, front, *extra, *arrays)
 
 
-def spread(value, pairs, receives):
-    got = lax.ppermute(value, ("row", "col"), pairs)
-    return jnp.where(receives, got, value)
+def spread(value, pairs):
+    return value + lax.ppermute(value, ("row", "col"), pairs)
 
 
 def share_panel(panel, part_cols):
@@ -151,14 +150,15 @@
     one_owner = part_rows % part_cols == 0
     groups = part_rows // part_cols if one_owner else 1
     count = 2 * groups
-    pieces = jnp.split(panel, count, axis=0)
+    held = jnp.where(me_col == 0, panel, jnp.zeros_like(panel))
+    pieces = lax.optimization_barrier(tuple(jnp.split(held, count, axis=0)))
     reach = n_col
     while reach > 1:
         half = reach // 2
         pairs = [
             (r * n_col + c, r * n_col + c + half) for r in range(n_row) for c in range(0, n_col, reach)
         ]
-        pieces = [spread(piece, pairs, me_col % reach == half) for piece in pieces]
+        pieces = [spread(piece, pairs) for piece in pieces]
         reach = half
     row_panel = jnp.concatenate(pieces, axis=0)
     if not one_owner:
@@ -169,8 +169,8 @@
         piece = pieces[k]
         for g in range(1, groups):
             piece = jnp.where(me_col % groups == g, pieces[2 * g + k], piece)
-        matching.append(piece)
-    away = (me_row - me_col // groups + n_row) % n_row
+        owner = me_row == me_col // groups
+        matching.append(jnp.where(owner, piece, jnp.zeros_like(piece)))
     reach = n_row
     while reach > 1:
         half = reach // 2
@@ -179,7 +179,7 @@
             for i in range(0, n_row, reach):
                 sender, receiver = (c // groups + i) % n_row, (c // groups + i + half) % n_row
                 pairs.append((sender * n_col + c, receiver * n_col + c))
-        matching = [spread(piece, pairs, away % reach == half) for piece in matching]
+        matching = [spread(piece, pairs) for piece in matching]
         reach = half
     return row_panel, jnp.concatenate(matching, axis=0)
 
@@ -237,7 +237,7 @@
         arrived = lax.all_to_all(outgoing, ("row", "col"), split_axis=0, concat_axis=0, tiled=True)
         incoming.append(arrived.reshape(n_row, n_col, row_cap * B, width * B))
 
-    group = largest_group(prb, 2)
+    group = largest_group(prb, 4)
     panel_to = jnp.minimum(col_to, PANEL_BLOCKS)
     local_panel = gather_call(
         functools.partial(panel_kernel, group, chunks[:1], n_col, col_cap),

time: 519 us -> 497 us (0.958)
  Pallas kernels: 105 us -> 87.9 us
    pallas_call x2, Pallas kernels: 59.7 us -> 50 us  [gather_call(): pl.pallas_call(body, grid_spec=pltpu.PrefetchScalarGridSpec(num_scalar_pr...]
    ppermute x10, waiting for transfers between devices: 205 us -> 198 us  [spread(): return value + lax.ppermute(value, ('row', 'col'), pairs)]
    pallas_call x2, Pallas kernels: 45 us -> 37.9 us  [pack(): pl.pallas_call(functools.partial(pack_kernel, group, n_col, col_cap, firs...]
  transfers between devices with their start and end apart: 12 -> 12, of which waited for: 7 -> 7; matrix products, arithmetic and copies ran while one was open for 1% -> 1% of each run, Pallas kernels for 8% -> 7%
where the time goes in v3:
time: 497 us; the launch traced here: 494 us
  waiting for transfers between devices  362 us (73%)
  Pallas kernels  87.9 us (18%)
  starting transfers between devices  32.1 us (6%)
  other arithmetic  8.22 us (2%)
    ppermute x10, waiting for transfers between devices, spread(): return value + lax.ppermute(value, ('row', 'col'), pairs)  198 us
    all_to_all x2, waiting for transfers between devices, local(): lax.all_to_all(outgoing, ('row', 'col'), split_axis=0, concat_axis=0, til...  165 us
    pallas_call x2, Pallas kernels, gather_call(): pl.pallas_call(body, grid_spec=pltpu.PrefetchScalarGridSpec(num_scalar_pr...  50 us
    pallas_call x2, Pallas kernels, pack(): pl.pallas_call(functools.partial(pack_kernel, group, n_col, col_cap, firs...  37.9 us
    ppermute x10, starting transfers between devices, spread(): return value + lax.ppermute(value, ('row', 'col'), pairs)  20.5 us
    all_to_all x2, starting transfers between devices, local(): lax.all_to_all(outgoing, ('row', 'col'), split_axis=0, concat_axis=0, til...  11.6 us
  transfers between devices with their start and end apart: 12, of which 7 were waited for; matrix products, arithmetic and copies ran while one was open for 1% of the time, Pallas kernels for 7%

profile of v3, /device:TPU:0, one launch (start us, length us, event | category | flops | bytes accessed | tf_op | source)
XLA Modules:
  0.0 493.8 jit_solution(9656956126716316912)
XLA Ops:
  0.6 0.8 reshape.119
  1.4 0.8 and_select_fusion
  2.9 19.0 %shard_map.59 = bf16[2,4,4096,256]{3,2,1,0:T(8,128)(2,1)} custom-call(s32[64]{0:T(128)S(1)} %select_reduce_fusion.row_src, s32[16]{0:T(128)S(1)} %select_reduce_fusion.2.col_src, bf16[8192,2048]{1,0:T(8,128)(2,1)} %refs_7_.3, bf16[8192,2048]{1,0:T(8,128)(2,1)} %refs_7_.3, bf16[8192,2048]{1,0:T(8,128)(2,1)} %refs_7_.3, bf16[8192,2048]{1,0:T(8,128)(2,1)} %refs_7_.3, ...), custom_call_target="tpu_custom_call" | custom-call | bytes 50331648 | tf_op jit(solution)/shard_map/pallas_call | solution.py:52
  21.9 5.8 %all-to-all-start = ((bf16[8,4096,256]{2,1,0:T(8,128)(2,1)}), bf16[8,4096,256]{2,1,0:T(8,128)(2,1)}, u32[]{:S(2)}, u32[]{:S(2)}) async-start(bf16[8,4096,256]{2,1,0:T(8,128)(2,1)} %bitcast.15), calls=%async_computation | async-start | bytes 33554432 | tf_op jit(solution)/shard_map/all_to_all | solution.py:237
  27.6 18.9 %shard_map.61 = bf16[2,4,4096,256]{3,2,1,0:T(8,128)(2,1)} custom-call(s32[64]{0:T(128)S(1)} %select_reduce_fusion.row_src, s32[16]{0:T(128)S(1)} %select_reduce_fusion.2.col_src, bf16[8192,2048]{1,0:T(8,128)(2,1)} %refs_7_.3, bf16[8192,2048]{1,0:T(8,128)(2,1)} %refs_7_.3, bf16[8192,2048]{1,0:T(8,128)(2,1)} %refs_7_.3, bf16[8192,2048]{1,0:T(8,128)(2,1)} %refs_7_.3, ...), custom_call_target="tpu_custom_call" | custom-call | bytes 50331648 | tf_op jit(solution)/shard_map/pallas_call | solution.py:52
  46.6 164.6 %all-to-all-done = bf16[8,4096,256]{2,1,0:T(8,128)(2,1)} async-done(((bf16[8,4096,256]{2,1,0:T(8,128)(2,1)}), bf16[8,4096,256]{2,1,0:T(8,128)(2,1)}, u32[]{:S(2)}, u32[]{:S(2)}) %all-to-all-start) | async-done | bytes 16777248 | tf_op jit(solution)/shard_map/all_to_all | solution.py:237
  211.2 5.9 %all-to-all-start.1 = ((bf16[8,4096,256]{2,1,0:T(8,128)(2,1)}), bf16[8,4096,256]{2,1,0:T(8,128)(2,1)}, u32[]{:S(2)}, u32[]{:S(2)}) async-start(bf16[8,4096,256]{2,1,0:T(8,128)(2,1)} %bitcast.14), calls=%async_computation.1 | async-start | bytes 33554432 | tf_op jit(solution)/shard_map/all_to_all | solution.py:237
  217.2 0.3 convert_reduce_fusion
  218.1 0.3 fusion.2
  218.3 14.1 %shard_map.60 = bf16[5120,256]{1,0:T(8,128)(2,1)S(1)} custom-call(s32[2,40]{1,0:T(2,128)S(1)} %get-tuple-element.12.src, s32[2,40]{1,0:T(2,128)S(1)} %get-tuple-element.11.slot, s32[2,40]{1,0:T(2,128)S(1)} %get-tuple-element.10.has_row, s32[2,16]{1,0:T(2,128)S(1)} %broadcast_minimum_fusion.col_to, bf16[5120,2560]{1,0:T(8,128)(2,1)} %refs_0_.7, ...), custom_call_target="tpu_custom_call" | custom-call | flops 671088640 | bytes 22020096 | tf_op jit(solution)/shard_map/pallas_call | solution.py:126
  232.8 3.7 collective-permute-start
  236.6 1.3 collective-permute-start.4
  237.9 1.3 collective-permute-start.2
  239.2 1.3 collective-permute-start.6
  240.6 164.3 %collective-permute-done = bf16[1280,256]{1,0:T(8,128)(2,1)S(1)} collective-permute-done((bf16[1280,256]{1,0:T(8,128)(2,1)S(1)}, bf16[1280,256]{1,0:T(8,128)(2,1)S(1)}, u32[]{:S(2)}, u32[]{:S(2)}) %collective-permute-start) | collective-permute-done | bytes 655392 | tf_op jit(solution)/shard_map/ppermute | solution.py:143
  405.1 1.3 collective-permute-start.1
  406.4 5.5 %collective-permute-done.4 = bf16[1280,256]{1,0:T(8,128)(2,1)S(1)} collective-permute-done((bf16[1280,256]{1,0:T(8,128)(2,1)S(1)}, bf16[1280,256]{1,0:T(8,128)(2,1)S(1)}, u32[]{:S(2)}, u32[]{:S(2)}) %collective-permute-start.4) | collective-permute-done | bytes 655392 | tf_op jit(solution)/shard_map/ppermute | solution.py:143
  412.1 2.1 collective-permute-start.5
  414.2 4.7 collective-permute-done.2
  419.1 2.1 collective-permute-start.3
  421.3 4.7 collective-permute-done.6
  426.1 2.2 collective-permute-start.7
  428.3 1.2 select_select_fusion.1
  429.6 3.6 collective-permute-start.8
  433.2 1.4 select_select_fusion
  434.7 1.3 collective-permute-start.9
  436.0 0.5 pad_maximum_fusion.refs_1_
  436.5 11.2 %collective-permute-done.8 = bf16[1280,256]{1,0:T(8,128)(2,1)S(1)} collective-permute-done((bf16[1280,256]{1,0:T(8,128)(2,1)S(1)}, bf16[1280,256]{1,0:T(8,128)(2,1)S(1)}, u32[]{:S(2)}, u32[]{:S(2)}) %collective-permute-start.8) | collective-permute-done | bytes 655392 | tf_op jit(solution)/shard_map/ppermute | solution.py:143
  448.0 7.3 %collective-permute-done.9 = bf16[1280,256]{1,0:T(8,128)(2,1)S(1)} collective-permute-done((bf16[1280,256]{1,0:T(8,128)(2,1)S(1)}, bf16[1280,256]{1,0:T(8,128)(2,1)S(1)}, u32[]{:S(2)}, u32[]{:S(2)}) %collective-permute-start.9) | collective-permute-done | bytes 655392 | tf_op jit(solution)/shard_map/ppermute | solution.py:143
  455.5 1.1 pad_maximum_fusion.1.refs_2_
  456.6 1.3 copy-done.1
  458.0 35.9 %shard_map.62 = bf16[5120,2560]{1,0:T(8,128)(2,1)} custom-call(s32[2,40]{1,0:T(2,128)S(1)} %get-tuple-element.12.src, s32[2,40]{1,0:T(2,128)S(1)} %get-tuple-element.11.slot, s32[2,40]{1,0:T(2,128)S(1)} %get-tuple-element.10.has_row, s32[2,16]{1,0:T(2,128)S(1)} %add.104.col_to, bf16[5120,2560]{1,0:T(8,128)(2,1)} %refs_0_.7, ...), custom_call_target="tpu_custom_call" | custom-call | flops 6710886400 | bytes 85983232 | tf_op jit(solution)/shard_map/pallas_call | solution.py:126
  (38 shorter events, 2.9 us)
Async XLA Ops:
  21.9 189.3 %all-to-all-start = ((bf16[8,4096,256]{2,1,0:T(8,128)(2,1)}), bf16[8,4096,256]{2,1,0:T(8,128)(2,1)}, u32[]{:S(2)}, u32[]{:S(2)}) async-start(bf16[8,4096,256]{2,1,0:T(8,128)(2,1)} %bitcast.15), calls=%async_computation | async-start | bytes 33554432 | tf_op jit(solution)/shard_map/all_to_all | solution.py:237
  211.2 5.9 %copy-start.3 = (s32[2,64]{1,0:T(2,128)S(1)}, s32[2,64]{1,0:T(2,128)}, u32[]{:S(2)}) copy-start(s32[2,64]{1,0:T(2,128)} %param.6) | copy-start | bytes 1540
  211.2 7.1 %copy-start.2 = (bf16[256,256]{1,0:T(8,128)(2,1)S(1)}, bf16[256,256]{1,0:T(8,128)(2,1)}, u32[]{:S(2)}) copy-start(bf16[256,256]{1,0:T(8,128)(2,1)} %refs_1_.4) | copy-start | bytes 393220
  211.2 245.4 %all-to-all-start.1 = ((bf16[8,4096,256]{2,1,0:T(8,128)(2,1)}), bf16[8,4096,256]{2,1,0:T(8,128)(2,1)}, u32[]{:S(2)}, u32[]{:S(2)}) async-start(bf16[8,4096,256]{2,1,0:T(8,128)(2,1)} %bitcast.14), calls=%async_computation.1 | async-start | bytes 33554432 | tf_op jit(solution)/shard_map/all_to_all | solution.py:237
  232.8 172.1 %collective-permute-start = (bf16[1280,256]{1,0:T(8,128)(2,1)S(1)}, bf16[1280,256]{1,0:T(8,128)(2,1)S(1)}, u32[]{:S(2)}, u32[]{:S(2)}) collective-permute-start(bf16[1280,256]{1,0:T(8,128)(2,1)S(1)} %get-tuple-element.6), channel_id=1, source_target_pairs={{0,2},{4,6},{8,10},{12,14},{16,18},{20,22},{24,26},{28,30}} | collective-permute-start | bytes 1966088 | tf_op jit(solution)/shard_map/ppermute | solution.py:143
  236.6 175.3 %collective-permute-start.4 = (bf16[1280,256]{1,0:T(8,128)(2,1)S(1)}, bf16[1280,256]{1,0:T(8,128)(2,1)S(1)}, u32[]{:S(2)}, u32[]{:S(2)}) collective-permute-start(bf16[1280,256]{1,0:T(8,128)(2,1)S(1)} %get-tuple-element.8), channel_id=1, source_target_pairs={{0,2},{4,6},{8,10},{12,14},{16,18},{20,22},{24,26},{28,30}} | collective-permute-start | bytes 1966088 | tf_op jit(solution)/shard_map/ppermute | solution.py:143
  237.9 181.0 %collective-permute-start.2 = (bf16[1280,256]{1,0:T(8,128)(2,1)S(1)}, bf16[1280,256]{1,0:T(8,128)(2,1)S(1)}, u32[]{:S(2)}, u32[]{:S(2)}) collective-permute-start(bf16[1280,256]{1,0:T(8,128)(2,1)S(1)} %get-tuple-element.7), channel_id=1, source_target_pairs={{0,2},{4,6},{8,10},{12,14},{16,18},{20,22},{24,26},{28,30}} | collective-permute-start | bytes 1966088 | tf_op jit(solution)/shard_map/ppermute | solution.py:143
  239.2 186.7 %collective-permute-start.6 = (bf16[1280,256]{1,0:T(8,128)(2,1)S(1)}, bf16[1280,256]{1,0:T(8,128)(2,1)S(1)}, u32[]{:S(2)}, u32[]{:S(2)}) collective-permute-start(bf16[1280,256]{1,0:T(8,128)(2,1)S(1)} %get-tuple-element.9), channel_id=1, source_target_pairs={{0,2},{4,6},{8,10},{12,14},{16,18},{20,22},{24,26},{28,30}} | collective-permute-start | bytes 1966088 | tf_op jit(solution)/shard_map/ppermute | solution.py:143
  405.1 23.2 %collective-permute-start.1 = (bf16[1280,256]{1,0:T(8,128)(2,1)S(1)}, bf16[1280,256]{1,0:T(8,128)(2,1)S(1)}, u32[]{:S(2)}, u32[]{:S(2)}) collective-permute-start(bf16[1280,256]{1,0:T(8,128)(2,1)S(1)} %add.110), channel_id=1, source_target_pairs={{0,1},{2,3},{4,5},{6,7},{8,9},{10,11},{12,13},{14,15},{16,17},{18,... | collective-permute-start | bytes 1966088 | tf_op jit(solution)/shard_map/ppermute | solution.py:143
  412.1 16.2 %collective-permute-start.5 = (bf16[1280,256]{1,0:T(8,128)(2,1)S(1)}, bf16[1280,256]{1,0:T(8,128)(2,1)}, u32[]{:S(2)}, u32[]{:S(2)}) collective-permute-start(bf16[1280,256]{1,0:T(8,128)(2,1)S(1)} %add.114), channel_id=1, source_target_pairs={{0,1},{2,3},{4,5},{6,7},{8,9},{10,11},{12,13},{14,15},{16,17},{18,... | collective-permute-start | bytes 1966088 | tf_op jit(solution)/shard_map/ppermute | solution.py:143
  419.1 14.1 %collective-permute-start.3 = (bf16[1280,256]{1,0:T(8,128)(2,1)S(1)}, bf16[1280,256]{1,0:T(8,128)(2,1)}, u32[]{:S(2)}, u32[]{:S(2)}) collective-permute-start(bf16[1280,256]{1,0:T(8,128)(2,1)S(1)} %add.112), channel_id=1, source_target_pairs={{0,1},{2,3},{4,5},{6,7},{8,9},{10,11},{12,13},{14,15},{16,17},{18,... | collective-permute-start | bytes 1966088 | tf_op jit(solution)/shard_map/ppermute | solution.py:143
  426.1 7.1 %collective-permute-start.7 = (bf16[1280,256]{1,0:T(8,128)(2,1)S(1)}, bf16[1280,256]{1,0:T(8,128)(2,1)}, u32[]{:S(2)}, u32[]{:S(2)}) collective-permute-start(bf16[1280,256]{1,0:T(8,128)(2,1)S(1)} %add.116), channel_id=1, source_target_pairs={{0,1},{2,3},{4,5},{6,7},{8,9},{10,11},{12,13},{14,15},{16,17},{18,... | collective-permute-start | bytes 1966088 | tf_op jit(solution)/shard_map/ppermute | solution.py:143
  429.6 18.2 %collective-permute-start.8 = (bf16[1280,256]{1,0:T(8,128)(2,1)S(1)}, bf16[1280,256]{1,0:T(8,128)(2,1)S(1)}, u32[]{:S(2)}, u32[]{:S(2)}) collective-permute-start(bf16[1280,256]{1,0:T(8,128)(2,1)S(1)} %get-tuple-element.13), channel_id=1, source_target_pairs={{0,4},{1,5},{6,2},{7,3},{8,12},{9,13},{14,10},{15,11},{16,20},{17,... | collective-permute-start | bytes 1966088 | tf_op jit(solution)/shard_map/ppermute | solution.py:143
  434.7 20.6 %collective-permute-start.9 = (bf16[1280,256]{1,0:T(8,128)(2,1)S(1)}, bf16[1280,256]{1,0:T(8,128)(2,1)S(1)}, u32[]{:S(2)}, u32[]{:S(2)}) collective-permute-start(bf16[1280,256]{1,0:T(8,128)(2,1)S(1)} %get-tuple-element.16), channel_id=1, source_target_pairs={{0,4},{1,5},{6,2},{7,3},{8,12},{9,13},{14,10},{15,11},{16,20},{17,... | collective-permute-start | bytes 1966088 | tf_op jit(solution)/shard_map/ppermute | solution.py:143
  436.5 20.1 %copy-start = (bf16[5120,256]{1,0:T(8,128)(2,1)}, bf16[5120,256]{1,0:T(8,128)(2,1)S(1)}, u32[]{:S(2)}) copy-start(bf16[5120,256]{1,0:T(8,128)(2,1)S(1)} %pad_maximum_fusion.refs_1_) | copy-start | bytes 7864324
  456.6 1.3 copy-start.1
